TPU v7x, 32 devices: a whole 2x2x4 slice. The times are simulated.
32 devices in a mesh: groups: 2 (over x), ep: 4 (over y, core), tp: 4 (over z).
Axes of the slice: x: 2, y: 2, z: 4, core: 2. Of those that a mesh axis runs over, the one named last changes fastest.
Arguments:
- tokens: bfloat16 [1024, 3584], P(('groups', 'ep')), parts along dimension 0, may hold values from -6 to 6
- expert_ids: int32 [1024, 8], P(('groups', 'ep')), parts along dimension 0, may hold values from 0 to 9, as said below
- route_weights: float32 [1024, 8], P(('groups', 'ep')), parts along dimension 0, may hold values from 0.05 to 1
- hot_list: int32 [4], P('groups'), parts along dimension 0, may hold values from 0 to 9, as said below
- cold_gate: bfloat16 [8, 3584, 1024], P('ep', None, 'tp'), may hold values from -0.09375 to 0.09375
- cold_up: bfloat16 [8, 3584, 1024], P('ep', None, 'tp'), may hold values from -0.09375 to 0.09375
- cold_down: bfloat16 [8, 1024, 3584], P('ep', 'tp'), may hold values from -0.1875 to 0.1875
- hot_gate: bfloat16 [2, 3584, 1024], P(None, None, 'tp'), may hold values from -0.09375 to 0.09375
- hot_up: bfloat16 [2, 3584, 1024], P(None, None, 'tp'), may hold values from -0.09375 to 0.09375
- hot_down: bfloat16 [2, 1024, 3584], P(None, 'tp'), may hold values from -0.1875 to 0.1875
Outputs:
- mixed: bfloat16 [1024, 3584], P(('groups', 'ep'), 'tp'), parts along dimension 0
There are 2 independent parts, one for each index of `groups`. A program takes and returns all parts, laid end to end along the dimension named above; an argument that names none is the same for every part. Nothing has to cross between parts.
Inputs may be any that keep to these rules, and one draw needn't show every extreme that they name: `expert_ids`: each row names 8 different experts. In each block of 128 rows (the tokens of one index of ep) no cold expert is named by more than 128 rows, and one cold expert, the same in every block, is named by exactly 128 rows. `hot_list`: 2 different expert ids in rising order; the last is always 10 - 1.
All inputs are finite; a program needn't handle non-finite values.
Results may differ from a plain program's by a relative error of at most 0.012.
Values may be sent and summed in bfloat16 or wider, within the bound.
A program may use at most 128 MiB of HBM per device.

v0:
```python
import jax
import jax.numpy as jnp
from jax import lax
from jax.sharding import PartitionSpec as P

ROUTE_SCALE = 2.5


def capacity_of(tok_rows, pick_count, hot_count, cold_count):
    cold_rows = tok_rows * pick_count - hot_count * (3 * tok_rows // 4)
    return min(2 * ((cold_rows + cold_count - 1) // cold_count), tok_rows)


def route_tables(pick_ids, weights, hot_list, cold_count, capacity):
    scaled = ROUTE_SCALE * weights / jnp.sum(weights, axis=1, keepdims=True)
    is_hot = pick_ids[:, :, None] == hot_list[None, None, :]
    hot_coef = jnp.sum(jnp.where(is_hot, scaled[:, :, None], jnp.float32(0.0)), axis=1)
    hot_below = jnp.sum((hot_list[None, None, :] < pick_ids[:, :, None]).astype(jnp.int32), axis=2)
    any_hot = jnp.any(is_hot, axis=2)
    cold_slot = jnp.where(any_hot, -1, pick_ids - hot_below)
    onehot = cold_slot[:, :, None] == jnp.arange(cold_count, dtype=jnp.int32)[None, None, :]
    per_token = jnp.sum(onehot.astype(jnp.int32), axis=1)
    before = jnp.cumsum(per_token, axis=0) - per_token
    pick_rank = jnp.sum(jnp.where(onehot, before[:, None, :], 0), axis=2)
    position = jnp.where(any_hot, -1, cold_slot * capacity + pick_rank)
    placed = (
        position[:, :, None] == jnp.arange(cold_count * capacity, dtype=jnp.int32)[None, None, :]
    )
    dispatch = jnp.any(placed, axis=1)
    combine = jnp.sum(jnp.where(placed, scaled[:, :, None], jnp.float32(0.0)), axis=1)
    return (hot_coef, dispatch, combine)


def per_device(
    tokens,
    expert_ids,
    route_weights,
    hot_list,
    cold_gate,
    cold_up,
    cold_down,
    hot_gate,
    hot_up,
    hot_down,
):
    tok_rows, model_width = tokens.shape
    local_cold = cold_gate.shape[0]
    ep_count = lax.axis_size("ep")
    cold_count = local_cold * ep_count
    capacity = capacity_of(tok_rows, expert_ids.shape[1], hot_list.shape[0], cold_count)
    hot_coef, dispatch, combine = route_tables(
        expert_ids, route_weights, hot_list, cold_count, capacity
    )
    buffer = jnp.einsum(
        "tr,td->rd", dispatch.astype(jnp.bfloat16), tokens, preferred_element_type=jnp.float32
    ).astype(jnp.bfloat16)
    buffer = buffer.reshape(ep_count, local_cold, capacity, model_width)
    slot_rows = lax.all_to_all(buffer, "ep", split_axis=0, concat_axis=0, tiled=True)
    gate_acts = jnp.einsum(
        "secd,edf->secf", slot_rows, cold_gate, preferred_element_type=jnp.float32
    )
    up_acts = jnp.einsum("secd,edf->secf", slot_rows, cold_up, preferred_element_type=jnp.float32)
    hidden = (jax.nn.silu(gate_acts) * up_acts).astype(jnp.bfloat16)
    partial_value = jnp.einsum(
        "secf,efd->secd", hidden, cold_down, preferred_element_type=jnp.float32
    )
    summed = lax.psum_scatter(
        partial_value.astype(jnp.bfloat16), "tp", scatter_dimension=3, tiled=True
    ).astype(jnp.float32)
    returned = lax.all_to_all(
        summed.astype(jnp.bfloat16), "ep", split_axis=0, concat_axis=0, tiled=True
    ).astype(summed.dtype)
    returned = returned.reshape(cold_count * capacity, returned.shape[3])
    cold_part = jnp.dot(
        combine, returned, precision=lax.Precision.HIGHEST, preferred_element_type=jnp.float32
    )
    hot_gate_acts = jnp.einsum("td,hdf->htf", tokens, hot_gate, preferred_element_type=jnp.float32)
    hot_up_acts = jnp.einsum("td,hdf->htf", tokens, hot_up, preferred_element_type=jnp.float32)
    hot_hidden = (jax.nn.silu(hot_gate_acts) * hot_up_acts).astype(jnp.bfloat16)
    hot_outputs = jnp.einsum(
        "htf,hfd->htd", hot_hidden, hot_down, preferred_element_type=jnp.float32
    )
    hot_partial = jnp.einsum("th,htd->td", hot_coef, hot_outputs, precision=lax.Precision.HIGHEST)
    hot_part = lax.psum_scatter(
        hot_partial.astype(jnp.bfloat16), "tp", scatter_dimension=1, tiled=True
    ).astype(jnp.float32)
    return (hot_part + cold_part).astype(jnp.bfloat16)


def solution(mesh):
    placed = (
        P(("groups", "ep"), None),
        P(("groups", "ep"), None),
        P(("groups", "ep"), None),
        P("groups"),
        P("ep", None, "tp"),
        P("ep", None, "tp"),
        P("ep", "tp", None),
        P(None, None, "tp"),
        P(None, None, "tp"),
        P(None, "tp", None),
    )
    return jax.shard_map(
        per_device, mesh=mesh, in_specs=placed, out_specs=P(("groups", "ep"), "tp"), check_vma=False
    )
```

profile of v0, /device:TPU:9, one launch (start us, length us, event | category | flops | bytes accessed | tf_op | source)
XLA Modules:
  0.0 309.5 jit_solution(4802145829229179749)
XLA Ops:
  6.5 0.0 copy-start
  6.5 0.0 reduce-scatter.9.cloned.1.call-start
  6.5 0.8 compare_reduce_fusion
  7.4 0.8 convert_reduce_fusion.1
  8.1 0.7 subtract_select_fusion
  8.9 0.1 copy.40
  9.0 0.2 reduce_window_sum.11
  9.2 0.1 copy.43
  9.3 1.3 fusion.5
  10.7 0.0 copy-done
  10.7 2.1 convolution_convert_fusion.1
  12.8 0.0 copy-start.5
  12.8 84.5 %all_to_all.10 = bf16[4,2,128,3584]{3,2,1,0:T(8,128)(2,1)S(1)} all-to-all(bf16[4,2,128,3584]{3,2,1,0:T(8,128)(2,1)S(1)} %bitcast.72), channel_id=1, replica_groups=mesh['groups'=2,'ep'=4,'tp'=4] {'ep'}, dimensions={0} | all-to-all | bytes 14680064 | tf_op jit(solution)/shard_map/all_to_all | solution.py:58
  97.3 0.0 copy-start.1
  97.3 3.0 copy-done.1
  100.3 0.0 copy-done.5
  100.3 2.0 fusion.11
  102.4 12.3 %fusion = bf16[4,2,128,3584]{3,2,0,1:T(8,128)(2,1)} fusion(bf16[2,256,3584]{2,1,0:T(8,128)(2,1)} %param.16, bf16[2,3584,256]{2,1,0:T(8,128)(2,1)} %param.15, bf16[4,2,128,3584]{3,2,1,0:T(8,128)(2,1)} %copy-done.1, f32[4,2,128,256]{3,2,0,1:T(8,128)S(1)} %fusion.11), kind=kOutput, calls=%fused_computation.2 | convolution fusion | flops 3763339264 | bytes 23068672 | tf_op jit(solution)/shard_map/secf,efd->secd/dot_general | solution.py:64
  114.6 12.2 %copy.59 = bf16[4,2,128,3584]{2,0,1,3:T(4,128)(2,1)} copy(bf16[4,2,128,3584]{3,2,0,1:T(8,128)(2,1)} %fusion) | data formatting | bytes 14680064
  126.9 12.6 %reshape.31 = bf16[3584,1024]{1,0:T(8,128)(2,1)} reshape(bf16[3584,2,4,128]{3,2,1,0:T(4,128)(2,1)} %bitcast.73) | data formatting | bytes 14680064
  139.5 0.0 copy-start.3
  139.5 0.0 copy-start.2
  139.5 0.0 copy-start.4
  139.5 0.0 reduce-scatter.9.cloned.1.call-update
  139.5 0.2 reduce-scatter.7.cloned.1.call-start
  139.8 0.4 copy-done.3
  140.2 0.0 copy-done.2
  140.2 0.0 copy-done.4
  140.2 0.1 fusion.54
  140.3 0.1 copy.51
  140.4 3.2 %convolution_bitcast_fusion.1 = f32[2,128,256]{1,2,0:T(8,128)S(1)} fusion(bf16[2,3584,256]{2,1,0:T(8,128)(2,1)} %param.17, bf16[128,3584]{1,0:T(8,128)(2,1)S(1)} %copy-done), kind=kOutput, calls=%fused_computation.24 | convolution fusion | flops 469762048 | bytes 4849664 | tf_op jit(solution)/shard_map/td,hdf->htf/dot_general | solution.py:77
  143.6 7.7 %fusion.38 = f32[2,128,3584]{2,1,0:T(8,128)} fusion(bf16[2,256,3584]{2,1,0:T(8,128)(2,1)} %param.19, bf16[2,3584,256]{2,1,0:T(8,128)(2,1)} %param.18, bf16[128,3584]{1,0:T(8,128)(2,1)S(1)} %copy-done, f32[2,128,256]{1,2,0:T(8,128)S(1)} %convolution_bitcast_fusion.1), kind=kOutput, calls=%fused_computation.26 | convolution fusion | flops 939917312 | bytes 12189696 | tf_op jit(solution)/shard_map/htf,hfd->htd/dot_general | solution.py:80
  151.3 18.9 %fusion.9 = bf16[128,1,3584]{2,1,0:T(2,128)(2,1)S(1)} fusion(f32[128,2,1]{1,2,0:T(1,128)S(1)} %copy.51, f32[2,128,3584]{2,1,0:T(8,128)} %fusion.38), kind=kOutput, calls=%fused_computation.13 | convolution fusion | flops 11010048 | bytes 4588544 | tf_op jit(solution)/shard_map/th,htd->td/dot_general | solution.py:83
  170.2 0.1 copy.79
  170.3 1.3 copy.57
  171.6 0.0 reduce-scatter.7.cloned.1.call-update
  171.6 96.5 %reduce-scatter.9.cloned.1.call-done = bf16[896,1024]{1,0:T(8,128)(2,1)} async-done(((bf16[3584,1024]{1,0:T(8,128)(2,1)}), bf16[896,1024]{1,0:T(8,128)(2,1)}) %reduce-scatter.9.cloned.1.call-update) | async-done | bytes 1835024
  268.1 3.6 %reshape.32 = bf16[896,2,4,128]{3,2,1,0:T(4,128)(2,1)S(1)} reshape(bf16[896,1024]{1,0:T(8,128)(2,1)} %reduce-scatter.9.cloned.1.call-done) | data formatting | bytes 3670016
  271.6 3.1 %copy.47 = bf16[4,2,128,896]{3,2,1,0:T(8,128)(2,1)} copy(bf16[4,2,128,896]{2,0,1,3:T(4,128)(2,1)S(1)} %bitcast.74) | data formatting | bytes 3670016 | tf_op jit(solution)/shard_map/reduce_scatter | solution.py:67
  274.8 4.2 %all-to-all-start.1 = ((bf16[4,2,128,896]{3,2,1,0:T(8,128)(2,1)}), bf16[4,2,128,896]{3,2,1,0:T(8,128)(2,1)S(1)}, u32[]{:S(2)}, u32[]{:S(2)}) async-start(bf16[4,2,128,896]{3,2,1,0:T(8,128)(2,1)} %copy.47), calls=%async_computation.1 | async-start | bytes 3670016 | tf_op jit(solution)/shard_map/all_to_all | solution.py:70
  279.0 0.1 copy.44
  279.1 1.3 select_reduce_fusion
  280.4 13.3 %reduce-scatter.7.cloned.1.call-done = bf16[896,128]{1,0:T(8,128)(2,1)} async-done(((bf16[3584,128]{1,0:T(8,128)(2,1)}), bf16[896,128]{1,0:T(8,128)(2,1)}) %reduce-scatter.7.cloned.1.call-update) | async-done | bytes 229392
  293.7 1.1 copy.58
  294.8 6.2 %all-to-all-done.1 = bf16[4,2,128,896]{3,2,1,0:T(8,128)(2,1)S(1)} async-done(((bf16[4,2,128,896]{3,2,1,0:T(8,128)(2,1)}), bf16[4,2,128,896]{3,2,1,0:T(8,128)(2,1)S(1)}, u32[]{:S(2)}, u32[]{:S(2)}) %all-to-all-start.1) | async-done | bytes 1835040 | tf_op jit(solution)/shard_map/all_to_all | solution.py:70
  301.0 1.7 fusion.35
  (7 shorter events, 0.1 us)
Async XLA Ops:
  6.5 4.1 %copy-start = (bf16[128,3584]{1,0:T(8,128)(2,1)S(1)}, bf16[128,3584]{1,0:T(8,128)(2,1)}, u32[]{:S(2)}) copy-start(bf16[128,3584]{1,0:T(8,128)(2,1)} %param.10) | copy-start | bytes 2752516
  6.5 261.5 %reduce-scatter.9.cloned.1.call-start = ((), (), s32[]{:S(2)}) async-start(), calls=%async_computation.5 | async-start | bytes 9175040
  12.8 87.5 %copy-start.5 = (bf16[2,3584,256]{2,1,0:T(8,128)(2,1)S(1)}, bf16[2,3584,256]{2,1,0:T(8,128)(2,1)}, u32[]{:S(2)}) copy-start(bf16[2,3584,256]{2,1,0:T(8,128)(2,1)} %param.14) | copy-start | bytes 11010052
  97.3 3.0 copy-start.1
  139.5 0.7 copy-start.3
  139.5 0.7 copy-start.2
  139.5 0.7 copy-start.4
  139.5 154.2 %reduce-scatter.7.cloned.1.call-start = ((), (), s32[]{:S(2)}) async-start(), calls=%async_computation.4 | async-start | bytes 1146880
  274.8 26.2 %all-to-all-start.1 = ((bf16[4,2,128,896]{3,2,1,0:T(8,128)(2,1)}), bf16[4,2,128,896]{3,2,1,0:T(8,128)(2,1)S(1)}, u32[]{:S(2)}, u32[]{:S(2)}) async-start(bf16[4,2,128,896]{3,2,1,0:T(8,128)(2,1)} %copy.47), calls=%async_computation.1 | async-start | bytes 3670016 | tf_op jit(solution)/shard_map/all_to_all | solution.py:70
Sparse Core Ops, SparseCore 0:
  139.7 128.3 reduce-scatter.8
  270.4 23.3 reduce-scatter.6
where the time goes:
time: 312 us; the launch traced here: 310 us
  waiting for transfers between devices  116 us (37%)
  blocking collectives  84.5 us (27%)
  matrix products  47.8 us (15%)
  local copies, waits for them, and re-layouts  38 us (12%)
  between operations  13.5 us (4%)
  other arithmetic  5.28 us (2%)
  starting transfers between devices  4.42 us (1%)
    unnamed x4, waiting for transfers between devices  110 us
    all_to_all x1, blocking collectives, per_device(): lax.all_to_all(buffer, 'ep', split_axis=0, concat_axis=0, tiled=True)  84.5 us
    unnamed x17, local copies, waits for them, and re-layouts  34.3 us
    dot_general x1, matrix products, per_device(): jnp.einsum('th,htd->td', hot_coef, hot_outputs, precision=lax.Precision.H...  18.9 us
    dot_general x1, matrix products, per_device(): jnp.einsum('secf,efd->secd', hidden, cold_down, preferred_element_type=jn...  12.3 us
    dot_general x1, matrix products, per_device(): jnp.einsum('htf,hfd->htd', hot_hidden, hot_down, preferred_element_type=j...  7.69 us
  transfers between devices with their start and end apart: 3, of which 3 were waited for; matrix products, arithmetic and copies ran while one was open for 13% of the time, Pallas kernels for 0%

commit v1 on v0

v1 whole, which is shorter than its diff:
```python
import functools

import jax
import jax.numpy as jnp
from jax import lax
from jax.experimental import pallas as pl
from jax.experimental.pallas import tpu as pltpu
from jax.sharding import PartitionSpec as P

ROUTE_SCALE = 2.5
MESH = pl.DeviceIdType.MESH
SPLITS = 4


def each(count, step):
    if count <= 4:
        for index in range(count):
            step(index)
    else:
        pl.loop(0, count)(step)


def layer_kernel(
    n_ep, n_tp,
    tok_hbm, ids_ref, weights_ref, hot_ref, cg, cu, cd, hg, hu, hd,
    out_ref,
    tok_all, wg, wu, vg, vu, wd, hid, hot_hid, coef_out, coef_in, part, own_part,
    core_out, core_in, y_out, y_in, z_out, z_in,
    w_sem, tok_sem, coef_sem, blk_sem, yt_sem, zt_sem, ct_sem, core_sem, y_sem, z_sem,
):
    rows, width = tok_hbm.shape
    cold, _, ff = wg.shape
    hot = vg.shape[0]
    piece = out_ref.shape[1]
    ny = n_ep // 2
    half = rows // 2
    run = half // SPLITS
    ep, tp = lax.axis_index("ep"), lax.axis_index("tp")
    y, c = ep // 2, ep % 2
    parity = tp % 2
    mate = y * 2 + (1 - c)
    pair = tp + 1 - 2 * parity

    barrier = pltpu.get_barrier_semaphore()

    def greet_ep(i):
        pl.semaphore_signal(
            barrier, inc=1, device_id={"ep": lax.rem(ep + 1 + i, n_ep)}, device_id_type=MESH
        )

    def greet_tp(i):
        pl.semaphore_signal(
            barrier, inc=1, device_id={"tp": lax.rem(tp + 1 + i, n_tp)}, device_id_type=MESH
        )

    each(n_ep - 1, greet_ep)
    each(n_tp - 1, greet_tp)

    own_rows = pl.ds(pl.multiple_of(c * rows, rows), rows)
    mate_rows = pl.ds(pl.multiple_of((1 - c) * rows, rows), rows)
    own_copy = pltpu.make_async_copy(tok_hbm, tok_all.at[y, own_rows], tok_sem.at[0])
    own_copy.start()
    loads = [
        pltpu.make_async_copy(src, dst, w_sem.at[i])
        for i, (src, dst) in enumerate([
            (hg, vg), (hu, vu), (cg, wg), (cu, wu),
            (cd, wd.at[pl.ds(0, cold * ff)]), (hd, wd.at[pl.ds(cold * ff, hot * ff)]),
        ])
    ]
    for load in loads:
        load.start()

    ids = ids_ref[...]
    weights = weights_ref[...]
    scaled = ROUTE_SCALE * weights / jnp.sum(weights, axis=1, keepdims=True)
    slot = ids
    hot_coef = []
    for h in range(hot):
        slot = slot - (hot_ref[h] < ids).astype(jnp.int32)
    for h in range(hot):
        match = ids == hot_ref[h]
        slot = jnp.where(match, -1, slot)
        hot_coef.append(jnp.sum(jnp.where(match, scaled, 0.0), axis=1, keepdims=True))
    lane = lax.broadcasted_iota(jnp.int32, (rows, 128), 1)
    lane_slot = jnp.where(lane % 8 < cold, (lane // 8) * cold + lane % 8, -2)
    table = jnp.zeros((rows, 128), jnp.float32)
    for k in range(ids.shape[1]):
        table = table + jnp.where(lane_slot == slot[:, k:k + 1], scaled[:, k:k + 1], 0.0)
    coef_out[...] = table.T

    def coef_rows(e):
        return pl.ds(pl.multiple_of(8 * e, 8), 8)

    pl.semaphore_wait(barrier, n_ep - 1 + n_tp - 1)

    def remote(src, dst, sems, *at, **target):
        return pltpu.make_async_remote_copy(
            src_ref=src, dst_ref=dst, send_sem=sems.at[(0, *at)], recv_sem=sems.at[(1, *at)],
            device_id=target, device_id_type=MESH,
        )

    def block_rows(core, which, s):
        return pl.ds(pl.multiple_of(core * rows + which * half + s * run, run), run)

    def tok_y(j, s):
        there = lax.rem(y + 1 + j, ny)
        return remote(
            tok_hbm.at[pl.ds(pl.multiple_of(parity * half + s * run, run), run)],
            tok_all.at[y, block_rows(c, parity, s)],
            yt_sem, j, s, ep=there * 2 + c,
        )

    def source(j):
        return lax.rem(y + ny - 1 - j, ny)

    def landed_y(j, s):
        at = tok_all.at[source(j), block_rows(c, parity, s)]
        return remote(at, at, yt_sem, j, s, ep=lax.rem(y + 1 + j, ny) * 2 + c)

    def tok_z(j, s):
        at = tok_all.at[source(j), block_rows(c, parity, s)]
        return remote(at, at, zt_sem, j, s, tp=pair)

    def landed_z(j, s):
        at = tok_all.at[source(j), block_rows(c, 1 - parity, s)]
        return remote(at, at, zt_sem, j, s, tp=pair)

    def tok_c(j, q, s):
        which = parity if q == 0 else 1 - parity
        at = tok_all.at[source(j), block_rows(c, which, s)]
        return remote(at, at, ct_sem, j, q, s, ep=mate)

    def landed_c(j, q, s):
        which = parity if q == 0 else 1 - parity
        at = tok_all.at[source(j), block_rows(1 - c, which, s)]
        return remote(at, at, ct_sem, j, q, s, ep=mate)

    def coef_copy(i):
        e = lax.rem(ep + 1 + i, n_ep)
        return remote(
            coef_out.at[coef_rows(e)], coef_in.at[coef_rows(ep)], coef_sem, i, ep=e
        )

    def landed_coef(i):
        e = lax.rem(ep + n_ep - 1 - i, n_ep)
        return remote(
            coef_out.at[coef_rows(e)], coef_in.at[coef_rows(e)], coef_sem, i,
            ep=lax.rem(ep + 1 + i, n_ep),
        )

    block_copy = remote(tok_hbm, tok_all.at[y, own_rows], blk_sem, 0, ep=mate)
    block_landed = remote(tok_hbm, tok_all.at[y, mate_rows], blk_sem, 0, ep=mate)

    for s in range(SPLITS):
        each(ny - 1, lambda j: tok_y(j, s).start())
    block_copy.start()
    each(n_ep - 1, lambda i: coef_copy(i).start())
    coef_in[coef_rows(ep), :] = coef_out[coef_rows(ep), :]

    def pass_on(s):
        def step(j):
            landed_y(j, s).wait_recv()
            tok_z(j, s).start()
            tok_c(j, 0, s).start()
        each(ny - 1, step)

    def pass_across(s):
        def step(j):
            landed_z(j, s).wait_recv()
            tok_c(j, 1, s).start()
        each(ny - 1, step)

    def act(x, gate, up, coef):
        g = jnp.dot(x, gate, preferred_element_type=jnp.float32)
        u = jnp.dot(x, up, preferred_element_type=jnp.float32)
        return (g / (1.0 + jnp.exp(-g)) * u * coef).astype(jnp.bfloat16)

    def cold_coef(yy, e):
        one = coef_in[coef_rows(yy * 2), :].T[:, e:e + 1]
        two = coef_in[coef_rows(yy * 2 + 1), :].T[:, e:e + 1]
        return jnp.concatenate([one, two], axis=0)

    def cold_hidden(yy, e):
        hid[yy, :, e * ff:(e + 1) * ff] = act(tok_all[yy], wg[e], wu[e], cold_coef(yy, e))

    own_copy.wait()
    loads[0].wait()
    loads[1].wait()
    for h in range(hot):
        hot_hid[:, h * ff:(h + 1) * ff] = act(
            tok_all[y, own_rows], vg[h], vu[h], hot_coef[h]
        )
    pass_on(0)
    loads[2].wait()
    loads[3].wait()
    block_landed.wait_recv()
    each(n_ep - 1, lambda i: landed_coef(i).wait_recv())
    for e in range(cold):
        cold_hidden(y, e)
        pass_on(1 + e)
        pass_across(e)
    for s in range(1 + cold, SPLITS):
        pass_on(s)
    for s in range(cold, SPLITS):
        pass_across(s)
    for s in range(SPLITS):
        each(ny - 1, lambda j: landed_c(j, 0, s).wait_recv())
    for s in range(SPLITS):
        each(ny - 1, lambda j: landed_c(j, 1, s).wait_recv())

    def far_hidden(j):
        for e in range(cold):
            cold_hidden(lax.rem(y + 1 + j, ny), e)

    each(ny - 1, far_hidden)
    loads[4].wait()
    loads[5].wait()

    def columns(k):
        t = lax.rem(tp + 1 + k, n_tp)
        return pl.ds(pl.multiple_of(t * piece, 128), piece)

    def core_copy(j, k):
        return remote(core_out.at[j, k], core_in.at[j, k], core_sem, j, k, ep=mate)

    def y_copy(j, k):
        return remote(
            y_out.at[j, k], y_in.at[j, k], y_sem, j, k, ep=lax.rem(y + 1 + j, ny) * 2 + c
        )

    def z_copy(k):
        return remote(z_out.at[k], z_in.at[k], z_sem, k, tp=lax.rem(tp + 1 + k, n_tp))

    def project(j, k):
        yy = lax.rem(y + 1 + j, ny)
        part[...] = jnp.dot(
            hid[yy], wd[:cold * ff, columns(k)], preferred_element_type=jnp.float32
        )
        core_out[j, k] = part[mate_rows, :].astype(jnp.bfloat16)
        core_copy(j, k).start()

    def far(k):
        def step(j):
            project(j, k)
            keep = part[own_rows, :]
            core_copy(j, k).wait_recv()
            y_out[j, k] = (keep + core_in[j, k].astype(jnp.float32)).astype(jnp.bfloat16)
            y_copy(j, k).start()
        each(ny - 1, step)

    each(n_tp, far)

    def near(k):
        project(ny - 1, k)
        own_part[k] = part[own_rows, :] + jnp.dot(
            hot_hid[...], wd[cold * ff:, columns(k)], preferred_element_type=jnp.float32
        )

    each(n_tp, near)

    def total(k):
        core_copy(ny - 1, k).wait_recv()
        own_part[k] += core_in[ny - 1, k].astype(jnp.float32)

        def step(j):
            y_copy(j, k).wait_recv()
            own_part[k] += y_in[j, k].astype(jnp.float32)
        each(ny - 1, step)

    def hand_on(k):
        total(k)
        z_out[k] = own_part[k].astype(jnp.bfloat16)
        z_copy(k).start()

    each(n_tp - 1, hand_on)
    total(n_tp - 1)

    def collect(k):
        z_copy(k).wait_recv()
        own_part[n_tp - 1] += z_in[k].astype(jnp.float32)

    each(n_tp - 1, collect)
    out_ref[...] = own_part[n_tp - 1].astype(out_ref.dtype)

    block_copy.wait_send()
    each(n_ep - 1, lambda i: coef_copy(i).wait_send())
    for s in range(SPLITS):
        def sent(j):
            tok_y(j, s).wait_send()
            tok_z(j, s).wait_send()
            tok_c(j, 0, s).wait_send()
            tok_c(j, 1, s).wait_send()
        each(ny - 1, sent)

    def sums_sent(k):
        each(ny, lambda j: core_copy(j, k).wait_send())
        each(ny - 1, lambda j: y_copy(j, k).wait_send())

    each(n_tp, sums_sent)
    each(n_tp - 1, lambda k: z_copy(k).wait_send())


def per_device(
    n_ep, n_tp,
    tokens, expert_ids, route_weights, hot_list,
    cold_gate, cold_up, cold_down, hot_gate, hot_up, hot_down,
):
    rows, width = tokens.shape
    cold, _, ff = cold_gate.shape
    hot = hot_gate.shape[0]
    ny = n_ep // 2
    piece = width // n_tp
    padded = -(-piece // 128) * 128

    def flat(down):
        down = down.reshape(-1, n_tp, piece)
        if padded != piece:
            down = jnp.pad(down, ((0, 0), (0, 0), (0, padded - piece)))
        return down.reshape(-1, n_tp * padded)

    bf16, f32 = jnp.bfloat16, jnp.float32
    dma = pltpu.SemaphoreType.DMA
    vmem = pl.BlockSpec(memory_space=pltpu.VMEM)
    hbm = pl.BlockSpec(memory_space=pl.ANY)
    out = pl.pallas_call(
        functools.partial(layer_kernel, n_ep, n_tp),
        out_shape=jax.ShapeDtypeStruct((rows, padded), bf16),
        in_specs=[hbm, vmem, vmem, pl.BlockSpec(memory_space=pltpu.SMEM)] + [hbm] * 6,
        out_specs=vmem,
        scratch_shapes=[
            pltpu.VMEM((ny, 2 * rows, width), bf16),
            pltpu.VMEM((cold, width, ff), bf16),
            pltpu.VMEM((cold, width, ff), bf16),
            pltpu.VMEM((hot, width, ff), bf16),
            pltpu.VMEM((hot, width, ff), bf16),
            pltpu.VMEM(((cold + hot) * ff, n_tp * padded), bf16),
            pltpu.VMEM((ny, 2 * rows, cold * ff), bf16),
            pltpu.VMEM((rows, hot * ff), bf16),
            pltpu.VMEM((128, rows), f32),
            pltpu.VMEM((128, rows), f32),
            pltpu.VMEM((2 * rows, padded), f32),
            pltpu.VMEM((n_tp, rows, padded), f32),
            pltpu.VMEM((ny, n_tp, rows, padded), bf16),
            pltpu.VMEM((ny, n_tp, rows, padded), bf16),
            pltpu.VMEM((ny - 1, n_tp, rows, padded), bf16),
            pltpu.VMEM((ny - 1, n_tp, rows, padded), bf16),
            pltpu.VMEM((n_tp - 1, rows, padded), bf16),
            pltpu.VMEM((n_tp - 1, rows, padded), bf16),
            dma((6,)),
            dma((1,)),
            dma((2, n_ep - 1)),
            dma((2, 1)),
            dma((2, ny - 1, SPLITS)),
            dma((2, ny - 1, SPLITS)),
            dma((2, ny - 1, 2, SPLITS)),
            dma((2, ny, n_tp)),
            dma((2, ny - 1, n_tp)),
            dma((2, n_tp - 1)),
        ],
        compiler_params=pltpu.CompilerParams(
            collective_id=0, has_side_effects=True, vmem_limit_bytes=63 * 1024 * 1024
        ),
        cost_estimate=pl.CostEstimate(
            flops=2 * rows * (n_ep * cold + hot) * 3 * width * ff,
            bytes_accessed=2 * 3 * (cold + hot) * width * ff,
            transcendentals=rows * (n_ep * cold + hot) * ff,
        ),
    )(
        tokens, expert_ids, route_weights, hot_list,
        cold_gate, cold_up, flat(cold_down), hot_gate, hot_up, flat(hot_down),
    )
    return out[:, :piece]


def solution(mesh):
    placed = (
        P(("groups", "ep"), None),
        P(("groups", "ep"), None),
        P(("groups", "ep"), None),
        P("groups"),
        P("ep", None, "tp"),
        P("ep", None, "tp"),
        P("ep", "tp", None),
        P(None, None, "tp"),
        P(None, None, "tp"),
        P(None, "tp", None),
    )
    return jax.shard_map(
        functools.partial(per_device, mesh.shape["ep"], mesh.shape["tp"]),
        mesh=mesh, in_specs=placed, out_specs=P(("groups", "ep"), "tp"), check_vma=False,
    )
```

time: 312 us -> 67.4 us (0.22)
  waiting for transfers between devices: 116 us -> 0 us
  blocking collectives: 84.5 us -> 0 us
  Pallas kernels: 0 us -> 62.6 us
  matrix products: 47.8 us -> 0 us
  local copies, waits for them, and re-layouts: 38 us -> 4.47 us
  between operations: 13.5 us -> 0.01 us
  other arithmetic: 5.28 us -> 0 us
  starting transfers between devices: 4.42 us -> 0 us
    unnamed x4 -> x0, waiting for transfers between devices: 110 us -> none
    all_to_all x1 -> x0, blocking collectives: 84.5 us -> none  [per_device(): lax.all_to_all(buffer, 'ep', split_axis=0, concat_axis=0, tiled=True)]
    pallas_call x0 -> x1, Pallas kernels: none -> 62.6 us  [per_device(): pl.pallas_call(functools.partial(layer_kernel, n_ep, n_tp), out_shape=jax...]
    dot_general x7 -> x0, matrix products: 47.8 us -> none  [the longest x1 18.9 us: per_device(): jnp.einsum('th,htd->td', hot_coef, hot_outputs, precision=lax.Precision.H...]
    unnamed x17 -> x3, local copies, waits for them, and re-layouts: 34.3 us -> 4.47 us
    all_to_all x1 -> x0, waiting for transfers between devices: 6.18 us -> none  [per_device(): lax.all_to_all(summed.astype(jnp.bfloat16), 'ep', split_axis=0, concat_ax...]
    all_to_all x1 -> x0, starting transfers between devices: 4.2 us -> none  [per_device(): lax.all_to_all(summed.astype(jnp.bfloat16), 'ep', split_axis=0, concat_ax...]
    reduce_scatter x1 -> x0, local copies, waits for them, and re-layouts: 3.14 us -> none  [per_device(): lax.psum_scatter(partial_value.astype(jnp.bfloat16), 'tp', scatter_dimens...]
  transfers between devices with their start and end apart: 3 -> 0, of which waited for: 3 -> 0; matrix products, arithmetic and copies ran while one was open for 13% -> 0% of each run, Pallas kernels for 0% -> 0%
where the time goes in v1:
time: 67.4 us; the launch traced here: 67.1 us
  Pallas kernels  62.6 us (93%)
  local copies, waits for them, and re-layouts  4.47 us (7%)
    pallas_call x1, Pallas kernels, per_device(): pl.pallas_call(functools.partial(layer_kernel, n_ep, n_tp), out_shape=jax...  62.6 us
    unnamed x3, local copies, waits for them, and re-layouts  4.47 us

profile of v1, /device:TPU:9, one launch (start us, length us, event | category | flops | bytes accessed | tf_op | source)
XLA Modules:
  0.0 67.1 jit_solution(4421317351743839707)
XLA Ops:
  0.0 1.4 %copy.11.ids_ref = s32[128,8]{1,0:T(8,128)} copy(s32[128,8]{0,1:T(8,128)} %param.11) | data formatting | bytes 8192 | tf_op args[1]
  1.4 1.4 %copy.12.weights_ref = f32[128,8]{1,0:T(8,128)} copy(f32[128,8]{0,1:T(8,128)} %param.12) | data formatting | bytes 8192 | tf_op args[2]
  2.8 62.6 %shard_map.100 = bf16[128,896]{1,0:T(8,128)(2,1)} custom-call(bf16[128,3584]{1,0:T(8,128)(2,1)} %tok_hbm.1, s32[128,8]{1,0:T(8,128)} %copy.11.ids_ref, f32[128,8]{1,0:T(8,128)} %copy.12.weights_ref, s32[2]{0:T(128)} %hot_ref.1, bf16[2,3584,256]{2,1,0:T(8,128)(2,1)} %cg.1, bf16[2,3584,256]{2,1,0:T(8,128)(2,1)} %cu.1, bf16[512,3584]{1,0:T(8,128)(2,1)} %bitcast.2, ...), custom_call_target="tpu_custom_call" | custom-call | flops 7046430720 | bytes 22020096 | tf_op jit(solution)/shard_map/pallas_call | solution.py:325
  65.5 1.6 %copy.14 = bf16[128,896]{1,0:T(8,128)(2,1)} copy(bf16[128,896]{1,0:T(8,128)(2,1)} %shard_map.100) | data formatting | bytes 458752

commit v2 on v1

--- a/solution.py
+++ b/solution.py
@@ -9,7 +9,8 @@
 
 ROUTE_SCALE = 2.5
 MESH = pl.DeviceIdType.MESH
-SPLITS = 4
+SPLITS = 2
+PARTS = 2
 
 
 def each(count, step):
@@ -70,8 +71,8 @@
     for load in loads:
         load.start()
 
-    ids = ids_ref[...]
-    weights = weights_ref[...]
+    ids = ids_ref[...].astype(jnp.float32).T.astype(jnp.int32)
+    weights = weights_ref[...].T
     scaled = ROUTE_SCALE * weights / jnp.sum(weights, axis=1, keepdims=True)
     slot = ids
     hot_coef = []
@@ -197,8 +198,10 @@
     each(n_ep - 1, lambda i: landed_coef(i).wait_recv())
     for e in range(cold):
         cold_hidden(y, e)
-        pass_on(1 + e)
-        pass_across(e)
+        if 1 + e < SPLITS:
+            pass_on(1 + e)
+        if e < SPLITS:
+            pass_across(e)
     for s in range(1 + cold, SPLITS):
         pass_on(s)
     for s in range(cold, SPLITS):
@@ -220,16 +223,26 @@
         t = lax.rem(tp + 1 + k, n_tp)
         return pl.ds(pl.multiple_of(t * piece, 128), piece)
 
-    def core_copy(j, k):
-        return remote(core_out.at[j, k], core_in.at[j, k], core_sem, j, k, ep=mate)
-
-    def y_copy(j, k):
-        return remote(
-            y_out.at[j, k], y_in.at[j, k], y_sem, j, k, ep=lax.rem(y + 1 + j, ny) * 2 + c
-        )
-
-    def z_copy(k):
-        return remote(z_out.at[k], z_in.at[k], z_sem, k, tp=lax.rem(tp + 1 + k, n_tp))
+    span = rows // PARTS
+
+    def cut(r):
+        return pl.ds(r * span, span)
+
+    def core_copy(j, k, r):
+        return remote(
+            core_out.at[j, k, cut(r)], core_in.at[j, k, cut(r)], core_sem, j, k, r, ep=mate
+        )
+
+    def y_copy(j, k, r):
+        return remote(
+            y_out.at[j, k, cut(r)], y_in.at[j, k, cut(r)], y_sem, j, k, r,
+            ep=lax.rem(y + 1 + j, ny) * 2 + c,
+        )
+
+    def z_copy(k, r):
+        return remote(
+            z_out.at[k, cut(r)], z_in.at[k, cut(r)], z_sem, k, r, tp=lax.rem(tp + 1 + k, n_tp)
+        )
 
     def project(j, k):
         yy = lax.rem(y + 1 + j, ny)
@@ -237,15 +250,19 @@
             hid[yy], wd[:cold * ff, columns(k)], preferred_element_type=jnp.float32
         )
         core_out[j, k] = part[mate_rows, :].astype(jnp.bfloat16)
-        core_copy(j, k).start()
+        for r in range(PARTS):
+            core_copy(j, k, r).start()
 
     def far(k):
         def step(j):
             project(j, k)
-            keep = part[own_rows, :]
-            core_copy(j, k).wait_recv()
-            y_out[j, k] = (keep + core_in[j, k].astype(jnp.float32)).astype(jnp.bfloat16)
-            y_copy(j, k).start()
+            for r in range(PARTS):
+                keep = part[pl.ds(pl.multiple_of(c * rows + r * span, span), span), :]
+                core_copy(j, k, r).wait_recv()
+                y_out[j, k, cut(r)] = (
+                    keep + core_in[j, k, cut(r)].astype(jnp.float32)
+                ).astype(jnp.bfloat16)
+                y_copy(j, k, r).start()
         each(ny - 1, step)
 
     each(n_tp, far)
@@ -258,26 +275,29 @@
 
     each(n_tp, near)
 
-    def total(k):
-        core_copy(ny - 1, k).wait_recv()
-        own_part[k] += core_in[ny - 1, k].astype(jnp.float32)
+    def total(k, r):
+        core_copy(ny - 1, k, r).wait_recv()
+        own_part[k, cut(r)] += core_in[ny - 1, k, cut(r)].astype(jnp.float32)
 
         def step(j):
-            y_copy(j, k).wait_recv()
-            own_part[k] += y_in[j, k].astype(jnp.float32)
+            y_copy(j, k, r).wait_recv()
+            own_part[k, cut(r)] += y_in[j, k, cut(r)].astype(jnp.float32)
         each(ny - 1, step)
 
     def hand_on(k):
-        total(k)
-        z_out[k] = own_part[k].astype(jnp.bfloat16)
-        z_copy(k).start()
+        for r in range(PARTS):
+            total(k, r)
+            z_out[k, cut(r)] = own_part[k, cut(r)].astype(jnp.bfloat16)
+            z_copy(k, r).start()
 
     each(n_tp - 1, hand_on)
-    total(n_tp - 1)
+    for r in range(PARTS):
+        total(n_tp - 1, r)
 
     def collect(k):
-        z_copy(k).wait_recv()
-        own_part[n_tp - 1] += z_in[k].astype(jnp.float32)
+        for r in range(PARTS):
+            z_copy(k, r).wait_recv()
+            own_part[n_tp - 1, cut(r)] += z_in[k, cut(r)].astype(jnp.float32)
 
     each(n_tp - 1, collect)
     out_ref[...] = own_part[n_tp - 1].astype(out_ref.dtype)
@@ -293,11 +313,13 @@
         each(ny - 1, sent)
 
     def sums_sent(k):
-        each(ny, lambda j: core_copy(j, k).wait_send())
-        each(ny - 1, lambda j: y_copy(j, k).wait_send())
+        for r in range(PARTS):
+            each(ny, lambda j: core_copy(j, k, r).wait_send())
+            each(ny - 1, lambda j: y_copy(j, k, r).wait_send())
 
     each(n_tp, sums_sent)
-    each(n_tp - 1, lambda k: z_copy(k).wait_send())
+    for r in range(PARTS):
+        each(n_tp - 1, lambda k: z_copy(k, r).wait_send())
 
 
 def per_device(
@@ -353,9 +375,9 @@
             dma((2, ny - 1, SPLITS)),
             dma((2, ny - 1, SPLITS)),
             dma((2, ny - 1, 2, SPLITS)),
-            dma((2, ny, n_tp)),
-            dma((2, ny - 1, n_tp)),
-            dma((2, n_tp - 1)),
+            dma((2, ny, n_tp, PARTS)),
+            dma((2, ny - 1, n_tp, PARTS)),
+            dma((2, n_tp - 1, PARTS)),
         ],
         compiler_params=pltpu.CompilerParams(
             collective_id=0, has_side_effects=True, vmem_limit_bytes=63 * 1024 * 1024
@@ -366,7 +388,7 @@
             transcendentals=rows * (n_ep * cold + hot) * ff,
         ),
     )(
-        tokens, expert_ids, route_weights, hot_list,
+        tokens, expert_ids.T, route_weights.T, hot_list,
         cold_gate, cold_up, flat(cold_down), hot_gate, hot_up, flat(hot_down),
     )
     return out[:, :piece]

time: 67.4 us -> 62.3 us (0.924)
  local copies, waits for them, and re-layouts: 4.47 us -> 1.65 us
  Pallas kernels: 62.6 us -> 60.4 us
    unnamed x3 -> x1, local copies, waits for them, and re-layouts: 4.47 us -> 1.65 us
    pallas_call x1, Pallas kernels: 62.6 us -> 60.4 us  [per_device(): pl.pallas_call(functools.partial(layer_kernel, n_ep, n_tp), out_shape=jax...]
where the time goes in v2:
time: 62.3 us; the launch traced here: 62.1 us
  Pallas kernels  60.4 us (97%)
  local copies, waits for them, and re-layouts  1.65 us (3%)
    pallas_call x1, Pallas kernels, per_device(): pl.pallas_call(functools.partial(layer_kernel, n_ep, n_tp), out_shape=jax...  60.4 us
    unnamed x1, local copies, waits for them, and re-layouts  1.65 us

profile of v2, /device:TPU:9, one launch (start us, length us, event | category | flops | bytes accessed | tf_op | source)
XLA Modules:
  0.0 62.1 jit_solution(14406802184883642966)
XLA Ops:
  0.0 60.4 %shard_map.100 = bf16[128,896]{1,0:T(8,128)(2,1)} custom-call(bf16[128,3584]{1,0:T(8,128)(2,1)} %tok_hbm.1, s32[8,128]{1,0:T(8,128)} %bitcast.6, f32[8,128]{1,0:T(8,128)} %bitcast.7, s32[2]{0:T(128)} %hot_ref.1, bf16[2,3584,256]{2,1,0:T(8,128)(2,1)} %cg.1, bf16[2,3584,256]{2,1,0:T(8,128)(2,1)} %cu.1, bf16[512,3584]{1,0:T(8,128)(2,1)} %bitcast.4, ...), custom_call_target="tpu_custom_call" | custom-call | flops 7046430720 | bytes 22020096 | tf_op jit(solution)/shard_map/pallas_call | solution.py:347
  60.4 1.6 %copy.12 = bf16[128,896]{1,0:T(8,128)(2,1)} copy(bf16[128,896]{1,0:T(8,128)(2,1)} %shard_map.100) | data formatting | bytes 458752

commit v3 on v2

--- a/solution.py
+++ b/solution.py
@@ -9,8 +9,9 @@
 
 ROUTE_SCALE = 2.5
 MESH = pl.DeviceIdType.MESH
-SPLITS = 2
+SPLITS = 4
 PARTS = 2
+FLIGHT = 2
 
 
 def each(count, step):
@@ -152,7 +153,7 @@
     block_copy = remote(tok_hbm, tok_all.at[y, own_rows], blk_sem, 0, ep=mate)
     block_landed = remote(tok_hbm, tok_all.at[y, mate_rows], blk_sem, 0, ep=mate)
 
-    for s in range(SPLITS):
+    for s in range(FLIGHT):
         each(ny - 1, lambda j: tok_y(j, s).start())
     block_copy.start()
     each(n_ep - 1, lambda i: coef_copy(i).start())
@@ -160,6 +161,9 @@
 
     def pass_on(s):
         def step(j):
+            if s + FLIGHT < SPLITS:
+                tok_y(j, s).wait_send()
+                tok_y(j, s + FLIGHT).start()
             landed_y(j, s).wait_recv()
             tok_z(j, s).start()
             tok_c(j, 0, s).start()
@@ -191,18 +195,20 @@
         hot_hid[:, h * ff:(h + 1) * ff] = act(
             tok_all[y, own_rows], vg[h], vu[h], hot_coef[h]
         )
-    pass_on(0)
+        if h < 2:
+            pass_on(h)
     loads[2].wait()
     loads[3].wait()
     block_landed.wait_recv()
     each(n_ep - 1, lambda i: landed_coef(i).wait_recv())
+    begun = min(hot, 2)
     for e in range(cold):
         cold_hidden(y, e)
-        if 1 + e < SPLITS:
-            pass_on(1 + e)
+        if begun + e < SPLITS:
+            pass_on(begun + e)
         if e < SPLITS:
             pass_across(e)
-    for s in range(1 + cold, SPLITS):
+    for s in range(begun + cold, SPLITS):
         pass_on(s)
     for s in range(cold, SPLITS):
         pass_across(s)
@@ -262,10 +268,14 @@
                 y_out[j, k, cut(r)] = (
                     keep + core_in[j, k, cut(r)].astype(jnp.float32)
                 ).astype(jnp.bfloat16)
-                y_copy(j, k, r).start()
         each(ny - 1, step)
 
-    each(n_tp, far)
+    def send_y(k, r):
+        def step(j):
+            if k > 0:
+                y_copy(j, k - 1, r).wait_send()
+            y_copy(j, k, r).start()
+        each(ny - 1, step)
 
     def near(k):
         project(ny - 1, k)
@@ -273,8 +283,6 @@
             hot_hid[...], wd[cold * ff:, columns(k)], preferred_element_type=jnp.float32
         )
 
-    each(n_tp, near)
-
     def total(k, r):
         core_copy(ny - 1, k, r).wait_recv()
         own_part[k, cut(r)] += core_in[ny - 1, k, cut(r)].astype(jnp.float32)
@@ -284,13 +292,23 @@
             own_part[k, cut(r)] += y_in[j, k, cut(r)].astype(jnp.float32)
         each(ny - 1, step)
 
-    def hand_on(k):
-        for r in range(PARTS):
-            total(k, r)
-            z_out[k, cut(r)] = own_part[k, cut(r)].astype(jnp.bfloat16)
-            z_copy(k, r).start()
-
-    each(n_tp - 1, hand_on)
+    def hand_on(k, r):
+        total(k, r)
+        z_out[k, cut(r)] = own_part[k, cut(r)].astype(jnp.bfloat16)
+        z_copy(k, r).start()
+
+    for k in range(n_tp):
+        far(k)
+        send_y(k, 0)
+        if k == 0:
+            for r in range(1, PARTS):
+                send_y(k, r)
+        near(k)
+        if k > 0:
+            hand_on(k - 1, 0)
+            for r in range(1, PARTS):
+                send_y(k, r)
+                hand_on(k - 1, r)
     for r in range(PARTS):
         total(n_tp - 1, r)
 
@@ -306,7 +324,8 @@
     each(n_ep - 1, lambda i: coef_copy(i).wait_send())
     for s in range(SPLITS):
         def sent(j):
-            tok_y(j, s).wait_send()
+            if s + FLIGHT >= SPLITS:
+                tok_y(j, s).wait_send()
             tok_z(j, s).wait_send()
             tok_c(j, 0, s).wait_send()
             tok_c(j, 1, s).wait_send()
@@ -315,10 +334,10 @@
     def sums_sent(k):
         for r in range(PARTS):
             each(ny, lambda j: core_copy(j, k, r).wait_send())
-            each(ny - 1, lambda j: y_copy(j, k, r).wait_send())
 
     each(n_tp, sums_sent)
     for r in range(PARTS):
+        each(ny - 1, lambda j: y_copy(j, n_tp - 1, r).wait_send())
         each(n_tp - 1, lambda k: z_copy(k, r).wait_send())
 
 

time: 62.3 us -> 57 us (0.915)
  Pallas kernels: 60.4 us -> 55.1 us
    pallas_call x1, Pallas kernels: 60.4 us -> 55.1 us  [per_device(): pl.pallas_call(functools.partial(layer_kernel, n_ep, n_tp), out_shape=jax...]
where the time goes in v3:
time: 57 us; the launch traced here: 56.8 us
  Pallas kernels  55.1 us (97%)
  local copies, waits for them, and re-layouts  1.65 us (3%)
    pallas_call x1, Pallas kernels, per_device(): pl.pallas_call(functools.partial(layer_kernel, n_ep, n_tp), out_shape=jax...  55.1 us
    unnamed x1, local copies, waits for them, and re-layouts  1.65 us

profile of v3, /device:TPU:9, one launch (start us, length us, event | category | flops | bytes accessed | tf_op | source)
XLA Modules:
  0.0 56.8 jit_solution(8669995735269499753)
XLA Ops:
  0.0 55.1 %shard_map.100 = bf16[128,896]{1,0:T(8,128)(2,1)} custom-call(bf16[128,3584]{1,0:T(8,128)(2,1)} %tok_hbm.1, s32[8,128]{1,0:T(8,128)} %bitcast.6, f32[8,128]{1,0:T(8,128)} %bitcast.7, s32[2]{0:T(128)} %hot_ref.1, bf16[2,3584,256]{2,1,0:T(8,128)(2,1)} %cg.1, bf16[2,3584,256]{2,1,0:T(8,128)(2,1)} %cu.1, bf16[512,3584]{1,0:T(8,128)(2,1)} %bitcast.4, ...), custom_call_target="tpu_custom_call" | custom-call | flops 7046430720 | bytes 22020096 | tf_op jit(solution)/shard_map/pallas_call | solution.py:366
  55.1 1.6 %copy.12 = bf16[128,896]{1,0:T(8,128)(2,1)} copy(bf16[128,896]{1,0:T(8,128)(2,1)} %shard_map.100) | data formatting | bytes 458752

commit v4 on v3

--- a/solution.py
+++ b/solution.py
@@ -72,6 +72,73 @@
     for load in loads:
         load.start()
 
+    def coef_rows(e):
+        return pl.ds(pl.multiple_of(8 * e, 8), 8)
+
+    pl.semaphore_wait(barrier, n_ep - 1 + n_tp - 1)
+
+    def remote(src, dst, sems, *at, **target):
+        return pltpu.make_async_remote_copy(
+            src_ref=src, dst_ref=dst, send_sem=sems.at[(0, *at)], recv_sem=sems.at[(1, *at)],
+            device_id=target, device_id_type=MESH,
+        )
+
+    def block_rows(core, which, s):
+        return pl.ds(pl.multiple_of(core * rows + which * half + s * run, run), run)
+
+    def tok_y(j, s):
+        there = lax.rem(y + 1 + j, ny)
+        return remote(
+            tok_hbm.at[pl.ds(pl.multiple_of(parity * half + s * run, run), run)],
+            tok_all.at[y, block_rows(c, parity, s)],
+            yt_sem, j, s, ep=there * 2 + c,
+        )
+
+    def source(j):
+        return lax.rem(y + ny - 1 - j, ny)
+
+    def landed_y(j, s):
+        at = tok_all.at[source(j), block_rows(c, parity, s)]
+        return remote(at, at, yt_sem, j, s, ep=lax.rem(y + 1 + j, ny) * 2 + c)
+
+    def tok_z(j, s):
+        at = tok_all.at[source(j), block_rows(c, parity, s)]
+        return remote(at, at, zt_sem, j, s, tp=pair)
+
+    def landed_z(j, s):
+        at = tok_all.at[source(j), block_rows(c, 1 - parity, s)]
+        return remote(at, at, zt_sem, j, s, tp=pair)
+
+    def tok_c(j, q, s):
+        which = parity if q == 0 else 1 - parity
+        at = tok_all.at[source(j), block_rows(c, which, s)]
+        return remote(at, at, ct_sem, j, q, s, ep=mate)
+
+    def landed_c(j, q, s):
+        which = parity if q == 0 else 1 - parity
+        at = tok_all.at[source(j), block_rows(1 - c, which, s)]
+        return remote(at, at, ct_sem, j, q, s, ep=mate)
+
+    def coef_copy(i):
+        e = lax.rem(ep + 1 + i, n_ep)
+        return remote(
+            coef_out.at[coef_rows(e)], coef_in.at[coef_rows(ep)], coef_sem, i, ep=e
+        )
+
+    def landed_coef(i):
+        e = lax.rem(ep + n_ep - 1 - i, n_ep)
+        return remote(
+            coef_out.at[coef_rows(e)], coef_in.at[coef_rows(e)], coef_sem, i,
+            ep=lax.rem(ep + 1 + i, n_ep),
+        )
+
+    block_copy = remote(tok_hbm, tok_all.at[y, own_rows], blk_sem, 0, ep=mate)
+    block_landed = remote(tok_hbm, tok_all.at[y, mate_rows], blk_sem, 0, ep=mate)
+
+    for s in range(FLIGHT):
+        each(ny - 1, lambda j: tok_y(j, s).start())
+    block_copy.start()
+
     ids = ids_ref[...].astype(jnp.float32).T.astype(jnp.int32)
     weights = weights_ref[...].T
     scaled = ROUTE_SCALE * weights / jnp.sum(weights, axis=1, keepdims=True)
@@ -90,72 +157,6 @@
         table = table + jnp.where(lane_slot == slot[:, k:k + 1], scaled[:, k:k + 1], 0.0)
     coef_out[...] = table.T
 
-    def coef_rows(e):
-        return pl.ds(pl.multiple_of(8 * e, 8), 8)
-
-    pl.semaphore_wait(barrier, n_ep - 1 + n_tp - 1)
-
-    def remote(src, dst, sems, *at, **target):
-        return pltpu.make_async_remote_copy(
-            src_ref=src, dst_ref=dst, send_sem=sems.at[(0, *at)], recv_sem=sems.at[(1, *at)],
-            device_id=target, device_id_type=MESH,
-        )
-
-    def block_rows(core, which, s):
-        return pl.ds(pl.multiple_of(core * rows + which * half + s * run, run), run)
-
-    def tok_y(j, s):
-        there = lax.rem(y + 1 + j, ny)
-        return remote(
-            tok_hbm.at[pl.ds(pl.multiple_of(parity * half + s * run, run), run)],
-            tok_all.at[y, block_rows(c, parity, s)],
-            yt_sem, j, s, ep=there * 2 + c,
-        )
-
-    def source(j):
-        return lax.rem(y + ny - 1 - j, ny)
-
-    def landed_y(j, s):
-        at = tok_all.at[source(j), block_rows(c, parity, s)]
-        return remote(at, at, yt_sem, j, s, ep=lax.rem(y + 1 + j, ny) * 2 + c)
-
-    def tok_z(j, s):
-        at = tok_all.at[source(j), block_rows(c, parity, s)]
-        return remote(at, at, zt_sem, j, s, tp=pair)
-
-    def landed_z(j, s):
-        at = tok_all.at[source(j), block_rows(c, 1 - parity, s)]
-        return remote(at, at, zt_sem, j, s, tp=pair)
-
-    def tok_c(j, q, s):
-        which = parity if q == 0 else 1 - parity
-        at = tok_all.at[source(j), block_rows(c, which, s)]
-        return remote(at, at, ct_sem, j, q, s, ep=mate)
-
-    def landed_c(j, q, s):
-        which = parity if q == 0 else 1 - parity
-        at = tok_all.at[source(j), block_rows(1 - c, which, s)]
-        return remote(at, at, ct_sem, j, q, s, ep=mate)
-
-    def coef_copy(i):
-        e = lax.rem(ep + 1 + i, n_ep)
-        return remote(
-            coef_out.at[coef_rows(e)], coef_in.at[coef_rows(ep)], coef_sem, i, ep=e
-        )
-
-    def landed_coef(i):
-        e = lax.rem(ep + n_ep - 1 - i, n_ep)
-        return remote(
-            coef_out.at[coef_rows(e)], coef_in.at[coef_rows(e)], coef_sem, i,
-            ep=lax.rem(ep + 1 + i, n_ep),
-        )
-
-    block_copy = remote(tok_hbm, tok_all.at[y, own_rows], blk_sem, 0, ep=mate)
-    block_landed = remote(tok_hbm, tok_all.at[y, mate_rows], blk_sem, 0, ep=mate)
-
-    for s in range(FLIGHT):
-        each(ny - 1, lambda j: tok_y(j, s).start())
-    block_copy.start()
     each(n_ep - 1, lambda i: coef_copy(i).start())
     coef_in[coef_rows(ep), :] = coef_out[coef_rows(ep), :]
 

time: 57 us -> 57 us (level)
  no operation moved by 1% of the time
where the time goes in v4:
time: 57 us; the launch traced here: 56.8 us
  Pallas kernels  55.1 us (97%)
  local copies, waits for them, and re-layouts  1.65 us (3%)
    pallas_call x1, Pallas kernels, per_device(): pl.pallas_call(functools.partial(layer_kernel, n_ep, n_tp), out_shape=jax...  55.1 us
    unnamed x1, local copies, waits for them, and re-layouts  1.65 us

profile of v4, /device:TPU:9, one launch (start us, length us, event | category | flops | bytes accessed | tf_op | source)
XLA Modules:
  0.0 56.8 jit_solution(6623406632880545399)
XLA Ops:
  0.0 55.1 %shard_map.100 = bf16[128,896]{1,0:T(8,128)(2,1)} custom-call(bf16[128,3584]{1,0:T(8,128)(2,1)} %tok_hbm.1, s32[8,128]{1,0:T(8,128)} %bitcast.6, f32[8,128]{1,0:T(8,128)} %bitcast.7, s32[2]{0:T(128)} %hot_ref.1, bf16[2,3584,256]{2,1,0:T(8,128)(2,1)} %cg.1, bf16[2,3584,256]{2,1,0:T(8,128)(2,1)} %cu.1, bf16[512,3584]{1,0:T(8,128)(2,1)} %bitcast.4, ...), custom_call_target="tpu_custom_call" | custom-call | flops 7046430720 | bytes 22020096 | tf_op jit(solution)/shard_map/pallas_call | solution.py:367
  55.1 1.6 %copy.12 = bf16[128,896]{1,0:T(8,128)(2,1)} copy(bf16[128,896]{1,0:T(8,128)(2,1)} %shard_map.100) | data formatting | bytes 458752
